TPU v7x, 32 devices: a whole 2x2x4 slice. The times are simulated.
32 devices in a mesh: parts: 2 (over x), dp: 16 (over z, y, core).
Axes of the slice: x: 2, y: 2, z: 4, core: 2. Of those that a mesh axis runs over, the one named last changes fastest.
Arguments:
- hidden_rows: bfloat16 [4096, 4096], P(('parts', 'dp')), parts along dimension 0, may hold values from -6 to 6
- queries: bfloat16 [4096, 4096], P(('parts', 'dp')), parts along dimension 0, may hold values from -0.5390625 to 0.5390625
- keys: bfloat16 [4096, 512], P(('parts', 'dp')), parts along dimension 0, may hold values from -6 to 6
- down_basis: bfloat16 [8192, 512], P('parts'), parts along dimension 0, may hold values from -0.09375 to 0.09375
- up_basis: bfloat16 [8, 128, 128], P('parts'), parts along dimension 0, may hold values from -0.5 to 0.5
- head_group: int32 [32], replicated, may hold values from 0 to 3, as said below
Outputs:
- down_new: bfloat16 [8192, 512], P(('parts', 'dp')), parts along dimension 0
- up_new: bfloat16 [8, 128, 128], P('parts'), parts along dimension 0
- row_error: float32 [4096], P(('parts', 'dp')), parts along dimension 0
There are 2 independent parts, one for each index of `parts`. A program takes and returns all parts, laid end to end along the dimension named above; an argument that names none is the same for every part. Nothing has to cross between parts.
Inputs may be any that keep to these rules, and one draw needn't show every extreme that they name: `head_group`: each of the 4 groups holds exactly 8 heads.
All inputs are finite; a program needn't handle non-finite values.
Results may differ from a plain program's by a relative error of at most 0.006.
Values may be sent and summed in bfloat16 or wider, within the bound.
A program may use at most 128 MiB of HBM per device.

v0:
```python
import math

import jax
import jax.numpy as jnp
from jax import lax
from jax.sharding import PartitionSpec as P

HEADS = 32
GROUPS = 4
HD = 128


PRECISE = lax.Precision.HIGHEST
RATE_DOWN = 1.0
RATE_UP = 8.0


def carried_in(part, axis, combine, identity):
    count = lax.axis_size(axis)
    place = lax.axis_index(axis)
    ahead = count - 1 - place
    gathered = lax.all_gather(part, axis)
    state = jnp.zeros_like(part) + jnp.asarray(identity, part.dtype)

    def one(turn, state):
        source = count - 1 - turn
        return combine(state, lax.dynamic_index_in_dim(gathered, source, 0, False))

    return lax.fori_loop(0, ahead, one, state)


def add_terms(earlier, later):
    return earlier + later


def shards(hidden_rows, queries, keys, down_basis, up_basis, head_group):
    tok_rows = hidden_rows.shape[0]
    devices = lax.axis_size("dp")
    my_index = lax.axis_index("dp")
    total_rows = tok_rows * devices
    width = GROUPS * HD
    pair_scale = 2.0 / (total_rows * total_rows * HEADS)
    root_tokens = math.sqrt(total_rows)
    part_rows = down_basis.shape[0] // devices
    select_f = (head_group[:, None] == jnp.arange(GROUPS, dtype=jnp.int32)[None, :]).astype(
        jnp.float32
    )
    select_b = select_f.astype(jnp.bfloat16)
    q_heads = queries.reshape(tok_rows, HEADS, HD)
    causal = jnp.arange(tok_rows)[:, None] >= jnp.arange(tok_rows)[None, :]
    q_positions = my_index * tok_rows + jnp.arange(tok_rows, dtype=jnp.int32)
    zero_gram = jnp.zeros((GROUPS, HD, HD), jnp.float32)
    head_gram = jnp.einsum("ihd,ihe->hde", q_heads, q_heads, preferred_element_type=jnp.float32)
    q_gram = jnp.einsum("hde,hg->gde", head_gram, select_f, precision=PRECISE)
    tail_gram = carried_in(q_gram, "dp", add_terms, zero_gram)

    def forward(down, up):
        latent = jnp.dot(hidden_rows, down, preferred_element_type=jnp.float32).astype(jnp.bfloat16)
        recon = jnp.einsum(
            "ngd,gde->nge",
            latent.reshape(tok_rows, GROUPS, HD),
            up,
            preferred_element_type=jnp.float32,
        )
        err_rows = (keys.reshape(tok_rows, GROUPS, HD).astype(jnp.float32) - recon).astype(
            jnp.bfloat16
        )
        e_heads = jnp.einsum(
            "jgd,hg->jhd", err_rows, select_b, preferred_element_type=jnp.float32
        ).astype(jnp.bfloat16)
        scores = jnp.einsum("ihd,jhd->hij", q_heads, e_heads, preferred_element_type=jnp.float32)
        scores = jnp.where(causal[None], scores, 0.0)
        return (latent, err_rows, scores)

    def update(down, up, latent, err_rows, scores):
        scores_b = scores.astype(jnp.bfloat16)
        local_part = jnp.einsum(
            "hij,ihd->jhd", scores_b, q_heads, preferred_element_type=jnp.float32
        )
        local_groups = jnp.einsum("jhd,hg->jgd", local_part, select_f, precision=PRECISE)
        cross_part = jnp.einsum(
            "jgd,gde->jge", err_rows.astype(jnp.float32), tail_gram, precision=PRECISE
        )
        grad_errs = (pair_scale * (local_groups + cross_part)).astype(jnp.bfloat16)
        latent_grad = (
            (-jnp.einsum("jge,gde->jgd", grad_errs, up, preferred_element_type=jnp.float32))
            .astype(jnp.bfloat16)
            .reshape(tok_rows, width)
        )
        up_local = -jnp.einsum(
            "jgd,jge->gde",
            latent.reshape(tok_rows, GROUPS, HD),
            grad_errs,
            preferred_element_type=jnp.float32,
        )
        up_grad = lax.psum(up_local, "dp")
        full_term = lax.dot_general(
            hidden_rows, latent_grad, (((0,), (0,)), ((), ())), preferred_element_type=jnp.float32
        )
        down_grad = lax.psum_scatter(full_term, "dp", scatter_dimension=0, tiled=True)
        own_rows = lax.dynamic_slice_in_dim(down, my_index * part_rows, part_rows, 0)
        new_rows = (own_rows.astype(jnp.float32) - RATE_DOWN * root_tokens * down_grad).astype(
            jnp.bfloat16
        )
        new_up = (up.astype(jnp.float32) - RATE_UP * root_tokens * up_grad).astype(jnp.bfloat16)
        return (new_rows, new_up)

    latent, err_rows, scores = forward(down_basis, up_basis)
    rows_one, up_one = update(down_basis, up_basis, latent, err_rows, scores)
    down_one = lax.all_gather(rows_one, "dp", axis=0, tiled=True)
    latent, err_rows, scores = forward(down_one, up_one)
    denominator = (q_positions + 1).astype(jnp.float32) * HEADS
    shard_piece = lax.all_gather(err_rows.reshape(tok_rows, width), "dp", axis=0, tiled=True)
    piece_len = shard_piece.shape[0]
    block_len = math.gcd(piece_len, 512)

    def one_block(block_idx, accum):
        block = lax.dynamic_slice_in_dim(shard_piece, block_idx * block_len, block_len, 0).reshape(
            block_len, GROUPS, HD
        )
        e_heads = jnp.einsum(
            "jgd,hg->jhd", block, select_b, preferred_element_type=jnp.float32
        ).astype(jnp.bfloat16)
        block_scores = jnp.einsum(
            "ihd,jhd->hij", q_heads, e_heads, preferred_element_type=jnp.float32
        )
        k_positions = block_idx * block_len + jnp.arange(block_len, dtype=jnp.int32)
        allowed = k_positions[None, :] <= q_positions[:, None]
        block_scores = jnp.where(allowed[None], block_scores, 0.0)
        return accum + jnp.sum(block_scores * block_scores, axis=(0, 2))

    totals = lax.fori_loop(
        0, piece_len // block_len, one_block, jnp.zeros((tok_rows,), jnp.float32)
    )
    row_error = totals / denominator
    rows_two, up_two = update(down_one, up_one, latent, err_rows, scores)
    return (rows_two, up_two, row_error)


def solution(mesh):
    return jax.shard_map(
        shards,
        mesh=mesh,
        in_specs=(
            P(("parts", "dp"), None),
            P(("parts", "dp"), None),
            P(("parts", "dp"), None),
            P("parts", None),
            P("parts", None, None),
            P(),
        ),
        out_specs=(P(("parts", "dp"), None), P("parts", None, None), P(("parts", "dp"))),
        check_vma=False,
    )
```

profile of v0, /device:TPU:0, one launch (start us, length us, event | category | flops | bytes accessed | tf_op | source)
XLA Modules:
  0.0 599.1 jit_solution(7190981767412222159)
XLA Ops:
  7.2 1.7 copy.86
  8.9 0.8 fusion.56
  9.8 2.0 fusion.18
  11.8 0.7 copy.94
  12.7 3.0 convolution_convert_fusion.3
  16.2 1.2 fusion.22
  17.4 2.8 convolution_bitcast_fusion.3
  20.2 3.5 fusion.20
  23.7 42.3 %all-gather.9.cloned.1.call-done = f32[64,128,128]{2,1,0:T(8,128)} async-done(((f32[4,128,128]{2,1,0:T(8,128)}), f32[64,128,128]{2,1,0:T(8,128)}) %all-gather.9.cloned.1.call-update) | async-done | bytes 4194320 | tf_op jit(solution)/shard_map/all_gather | solution.py:22
  65.9 15.5 %while.26 = (s32[]{:T(128)}, f32[4,128,128]{2,1,0:T(8,128)S(1)}, s32[]{:T(128)}, f32[16,4,128,128]{3,2,1,0:T(8,128)}, s32[]{:T(128)}, /*index=5*/s32[]{:T(128)}, s32[]{:T(128)}, s32[]{:T(128)}) while((s32[]{:T(128)}, f32[4,128,128]{2,1,0:T(8,128)S(1)}, s32[]{:T(128)}, f32[16,4,128,128]{3,2,1,0:T(8,128)}, s32[]{:T(128)}, /*index=5*/s32[]{:T(128)}, ...), condition=%wide.region_1.2_spmd, body=%wide.region_0.1_spmd.sunk | while | flops 65542 | bytes 786575 | solution.py:29
  66.0 1.0 bitcast_add_fusion.2
  67.0 1.0 bitcast_add_fusion.2
  68.0 1.0 bitcast_add_fusion.2
  69.1 1.0 bitcast_add_fusion.2
  70.1 1.0 bitcast_add_fusion.2
  71.1 1.0 bitcast_add_fusion.2
  72.2 1.0 bitcast_add_fusion.2
  73.2 1.0 bitcast_add_fusion.2
  74.2 1.0 bitcast_add_fusion.2
  75.3 1.0 bitcast_add_fusion.2
  76.3 1.0 bitcast_add_fusion.2
  77.3 1.0 bitcast_add_fusion.2
  78.4 1.0 bitcast_add_fusion.2
  79.4 1.0 bitcast_add_fusion.2
  80.4 1.0 bitcast_add_fusion.2
  82.0 4.5 convolution_bitcast_fusion.1
  86.5 1.0 constant_dynamic-slice_fusion.1
  87.6 0.9 convolution_negate_fusion.2
  88.6 100.1 %reduce-scatter.3.cloned.1.call-done = f32[256,512]{0,1:T(8,128)} async-done(((f32[4096,512]{0,1:T(8,128)}), f32[256,512]{0,1:T(8,128)}) %reduce-scatter.3.cloned.1.call-update) | async-done | bytes 524304 | tf_op jit(solution)/shard_map/reduce_scatter | solution.py:100
  188.7 1.8 subtract_convert_fusion.1
  190.8 90.5 %all-reduce.3.cloned.1.call-done = f32[4,128,128]{2,1,0:T(8,128)} async-done(((f32[4,128,128]{2,1,0:T(8,128)}), f32[4,128,128]{2,1,0:T(8,128)}) %all-reduce.3.cloned.1.call-update) | async-done | bytes 262160 | tf_op jit(solution)/shard_map/psum | solution.py:96
  281.2 1.0 subtract_convert_fusion.3
  282.3 54.8 %all-gather.5.cloned.1.call-done = bf16[4096,512]{0,1:T(8,128)(2,1)} async-done(((bf16[256,512]{0,1:T(8,128)(2,1)}), bf16[4096,512]{0,1:T(8,128)(2,1)}) %all-gather.5.cloned.1.call-update) | async-done | bytes 4194320 | tf_op jit(solution)/shard_map/all_gather | solution.py:110
  337.0 3.4 convolution_convert_fusion.2
  340.7 0.4 copy-done.6
  341.1 0.6 copy-done.1
  341.8 0.8 copy.100
  342.5 1.4 fusion.23
  344.0 2.8 convolution_bitcast_fusion.2
  346.8 3.5 fusion.16
  350.6 0.9 convolution_negate_fusion
  351.5 0.5 all-gather.7.cloned.1.call-update
  352.3 4.5 convolution_bitcast_fusion
  356.9 0.7 copy.110
  357.5 81.1 %all-reduce.5.cloned.1.call-done = f32[4,128,128]{2,1,0:T(8,128)} async-done(((f32[4,128,128]{2,1,0:T(8,128)}), f32[4,128,128]{2,1,0:T(8,128)}) %all-reduce.5.cloned.1.call-update) | async-done | bytes 262160 | tf_op jit(solution)/shard_map/psum | solution.py:96
  438.6 1.6 subtract_convert_fusion.2
  440.3 42.1 %all-gather.7.cloned.1.call-done = bf16[2048,512]{0,1:T(8,128)(2,1)} async-done(((bf16[128,512]{0,1:T(8,128)(2,1)}), bf16[2048,512]{0,1:T(8,128)(2,1)}) %all-gather.7.cloned.1.call-update) | async-done | bytes 2097168 | tf_op jit(solution)/shard_map/all_gather | solution.py:113
  482.4 30.2 %while.27 = (s32[]{:T(128)}, f32[128]{0:T(128)S(1)}, bf16[2048,512]{0,1:T(8,128)(2,1)}, bf16[128,32,128]{2,0,1:T(8,128)(2,1)S(1)}, s32[]{:T(128)}, /*index=5*/s3...) while((s32[]{:T(128)}, f32[128]{0:T(128)S(1)}, bf16[2048,512]{0,1:T(8,128)(2,1)}, ...), condition=%wide.region_8.9_spmd.clone, body=%wide.region_6.8_spmd.clone.sunk | while | flops 562103424 | bytes 12197169 | solution.py:132
  482.5 1.1 constant_dynamic-slice_fusion.3
  483.9 1.3 convert_bitcast_fusion.2
  485.2 4.6 fusion.100
  490.0 1.2 constant_dynamic-slice_fusion.3
  491.5 1.3 convert_bitcast_fusion.2
  492.8 4.6 fusion.100
  497.6 1.2 constant_dynamic-slice_fusion.3
  499.1 1.3 convert_bitcast_fusion.2
  500.4 4.6 fusion.100
  505.2 1.2 constant_dynamic-slice_fusion.3
  506.7 1.3 convert_bitcast_fusion.2
  508.0 4.6 fusion.100
  512.6 0.5 multiply_divide_fusion
  513.1 77.1 %reduce-scatter.5.cloned.1.call-done = f32[256,512]{0,1:T(8,128)} async-done(((f32[4096,512]{0,1:T(8,128)}), f32[256,512]{0,1:T(8,128)}) %reduce-scatter.5.cloned.1.call-update) | async-done | bytes 524304 | tf_op jit(solution)/shard_map/reduce_scatter | solution.py:100
  590.2 1.2 subtract_convert_fusion
  591.4 0.8 copy.111
  (66 shorter events, 4.5 us)
Async XLA Ops:
  7.2 5.5 copy-start
  7.2 58.7 %all-gather.9.cloned.1.call-start = ((), (), s32[]{:S(2)}) async-start(), calls=%async_computation.8 | async-start | bytes 4456448 | tf_op jit(solution)/shard_map/all_gather | solution.py:22
  8.9 0.9 copy-start.9
  9.8 2.8 copy-start.8
  12.5 176.2 %reduce-scatter.3.cloned.1.call-start = ((), (), s32[]{:S(2)}) async-start(), calls=%async_computation.2 | async-start | bytes 8912896 | tf_op jit(solution)/shard_map/reduce_scatter | solution.py:100
  12.7 3.1 copy-start.4
  12.7 3.3 copy-start.3
  86.5 194.8 %all-reduce.3.cloned.1.call-start = ((), (), s32[]{:S(2)}) async-start(), calls=%async_computation.4 | async-start | bytes 524288 | tf_op jit(solution)/shard_map/psum | solution.py:96
  88.5 248.5 %all-gather.5.cloned.1.call-start = ((), (), s32[]{:S(2)}) async-start(), calls=%async_computation.3 | async-start | bytes 4456448 | tf_op jit(solution)/shard_map/all_gather | solution.py:110
  190.5 248.1 %all-reduce.5.cloned.1.call-start = ((), (), s32[]{:S(2)}) async-start(), calls=%async_computation.6 | async-start | bytes 524288 | tf_op jit(solution)/shard_map/psum | solution.py:96
  282.2 58.2 %copy-start.5 = (bf16[128,512]{0,1:T(8,128)(2,1)S(1)}, bf16[128,512]{0,1:T(8,128)(2,1)}, u32[]{:S(2)}) copy-start(bf16[128,512]{0,1:T(8,128)(2,1)} %copy-done.4) | copy-start | bytes 393220
  340.4 0.7 copy-start.6
  341.1 0.6 copy-start.1
  346.7 3.5 copy-start.2
  346.7 3.8 copy-start.7
  351.5 130.9 %all-gather.7.cloned.1.call-start = ((), (), s32[]{:S(2)}) async-start(), calls=%async_computation.7 | async-start | bytes 2228224 | tf_op jit(solution)/shard_map/all_gather | solution.py:113
  352.1 238.1 %reduce-scatter.5.cloned.1.call-start = ((), (), s32[]{:S(2)}) async-start(), calls=%async_computation.5 | async-start | bytes 8912896 | tf_op jit(solution)/shard_map/reduce_scatter | solution.py:100
  356.8 125.5 %copy-start.10 = (s32[32]{0:T(128)S(1)}, s32[32]{0:T(128)}, u32[]{:S(2)}) copy-start(s32[32]{0:T(128)} %param.15) | copy-start | bytes 388
Sparse Core Ops, SparseCore 0:
  12.6 53.2 all-gather.8
  86.6 102.0 reduce-scatter.2
  192.7 88.5 all-reduce.2
  283.3 53.6 all-gather.4
  351.6 86.9 all-reduce.4
  440.6 41.6 all-gather.6
  486.4 103.7 reduce-scatter.4
where the time goes:
time: 600 us; the launch traced here: 599 us
  waiting for transfers between devices  488 us (81%)
  matrix products  60 us (10%)
  other arithmetic  21.9 us (4%)
  between operations  14.4 us (2%)
  local copies, waits for them, and re-layouts  13.2 us (2%)
    reduce_scatter x2, waiting for transfers between devices, update(): lax.psum_scatter(full_term, 'dp', scatter_dimension=0, tiled=True)  177 us
    psum x2, waiting for transfers between devices, update(): up_grad = lax.psum(up_local, 'dp')  172 us
    all_gather x1, waiting for transfers between devices, shards(): down_one = lax.all_gather(rows_one, 'dp', axis=0, tiled=True)  54.8 us
    all_gather x1, waiting for transfers between devices, carried_in(): gathered = lax.all_gather(part, axis)  42.3 us
    all_gather x1, waiting for transfers between devices, shards(): lax.all_gather(err_rows.reshape(tok_rows, width), 'dp', axis=0, tiled=True)  42.1 us
    dot_general x4, matrix products, one_block(): jnp.einsum('ihd,jhd->hij', q_heads, e_heads, preferred_element_type=jnp.f...  18.4 us
    add x15, other arithmetic, add_terms(): return earlier + later  15.2 us
  transfers between devices with their start and end apart: 7, of which 7 were waited for; matrix products, arithmetic and copies ran while one was open for 9% of the time, Pallas kernels for 0%

commit v1 on v0

v1 whole, which is shorter than its diff:
```python
import functools
import math

import jax
import jax.numpy as jnp
from jax import lax
from jax.experimental import pallas as pl
from jax.experimental.pallas import tpu as pltpu
from jax.sharding import PartitionSpec as P

HEADS = 32
GROUPS = 4
HD = 128
PER = HEADS // GROUPS
WIDTH = GROUPS * HD
RATE_DOWN = 1.0
RATE_UP = 8.0
F32 = jnp.float32
BF16 = jnp.bfloat16
MESH = pl.DeviceIdType.MESH


def mm(a, b, dims=((1,), (0,))):
    return lax.dot_general(a, b, (dims, ((), ())), preferred_element_type=F32)


def split(x):
    hi = x.astype(BF16)
    return hi, (x - hi.astype(F32)).astype(BF16)


def sort_heads(order, queries, qs):
    tok = queries.shape[0]
    for s in range(HEADS):
        col = pl.multiple_of(order[s] * HD, HD)
        qs[s * tok:(s + 1) * tok] = queries[:, pl.ds(col, HD)]


def kernel(
    n, tok, feat,
    hid, qs, keys, down0, up0,
    rows_out, up_out, err_out,
    hid_t, feats, latent_b, gl1, gl2, down1, gram, kgram, upl1, upl2,
    stages, results, finals,
    a2a_s, a2a_r, p1_s, p1_r, p2_s, p2_r, agz_s, agy_s, agc_s, ag_r,
):
    me = lax.axis_index("dp")
    planes = n // 4
    zi, yi, ci = me // 4, (me // 2) % 2, me % 2
    ypeer = zi * 4 + (1 - yi) * 2 + ci
    cpeer = zi * 4 + yi * 2 + (1 - ci)
    part = feat // n
    piece = WIDTH // n
    total = n * tok
    pair_scale = 2.0 / (total * total * HEADS)
    root = math.sqrt(total)

    def remote(src, dst, s, r, to):
        return pltpu.make_async_remote_copy(
            src_ref=src, dst_ref=dst, send_sem=s, recv_sem=r,
            device_id={"dp": to}, device_id_type=MESH,
        )

    def peers(body):
        def one(k, carry):
            body(lax.rem(me + k, n))
            return carry

        lax.fori_loop(1, n, one, 0)

    def phase1_desc(u, src, owner, to):
        return remote(
            src.at[pl.ds(pl.multiple_of(to * piece, piece), piece)],
            stages.at[u, owner], p1_s.at[u, to], p1_r.at[u, owner], to,
        )

    def phase1_start(u, src):
        peers(lambda p: phase1_desc(u, src, me, p).start())
        stages[u, me] = src[pl.ds(pl.multiple_of(me * piece, piece), piece)]

    def phase2_desc(u, owner, to):
        return remote(
            results.at[u, to],
            finals.at[u, pl.ds(pl.multiple_of(owner * piece, piece), piece)],
            p2_s.at[u, to], p2_r.at[u, owner], to,
        )

    def phase2_start(u, src, mode):
        peers(lambda p: phase1_desc(u, src, p, p).wait_recv())
        zero = jnp.zeros((piece, HD), F32)
        if mode == "sum":
            tot = lax.fori_loop(0, n, lambda k, a: a + stages[u, k], zero)

            def put(k, carry):
                results[u, k] = tot
                return carry

            lax.fori_loop(0, n, put, 0)
        else:
            def scan(k, a):
                at = n - 1 - k if mode == "suffix" else k
                results[u, at] = a
                return a + stages[u, at]

            lax.fori_loop(0, n, scan, zero)
        peers(lambda p: phase2_desc(u, me, p).start())
        finals[u, pl.ds(pl.multiple_of(me * piece, piece), piece)] = results[u, me]

    def phase2_wait(u):
        peers(lambda p: phase2_desc(u, p, p).wait_recv())

    def exchange_sends_done(u, src):
        peers(lambda p: phase1_desc(u, src, me, p).wait_send())
        peers(lambda p: phase2_desc(u, me, p).wait_send())

    def blk(buf, rows, b):
        return buf.at[pl.ds(pl.multiple_of(b * rows, rows), rows)]

    def ag_desc(u, buf, rows, b, to, sem):
        ref = blk(buf, rows, b)
        return remote(ref, ref, sem, ag_r.at[u, b], to)

    def zblock(k):
        return lax.rem(zi + k, planes) * 4 + yi * 2 + ci

    def yblock(k):
        return lax.rem(zi + k, planes) * 4 + (1 - yi) * 2 + ci

    def gather(u, buf, rows):
        def loop(lo, hi, body):
            def one(k, carry):
                body(k)
                return carry

            lax.fori_loop(lo, hi, one, 0)

        def arrived(b):
            ag_desc(u, buf, rows, b, b, agy_s.at[u, b]).wait_recv()

        def to_z(k):
            ag_desc(u, buf, rows, me, zblock(k), agz_s.at[u, k]).start()

        def to_y(b):
            ag_desc(u, buf, rows, b, ypeer, agy_s.at[u, b]).start()

        def to_c(b):
            ag_desc(u, buf, rows, b, cpeer, agc_s.at[u, b]).start()

        loop(1, planes, to_z)
        to_y(me)
        to_c(me)

        def from_z(k):
            b = zblock(k)
            arrived(b)
            to_y(b)
            to_c(b)

        loop(1, planes, from_z)

        def from_y(k):
            b = yblock(k)
            arrived(b)
            to_c(b)

        loop(0, planes, from_y)

        def from_c(k):
            arrived(lax.rem(zi + k // 2, planes) * 4 + lax.rem(k, 2) * 2 + (1 - ci))

        loop(0, 2 * planes, from_c)

    def gather_sends_done(u, buf, rows):
        def z(k, carry):
            ag_desc(u, buf, rows, me, zblock(k), agz_s.at[u, k]).wait_send()
            return carry

        lax.fori_loop(1, planes, z, 0)

        def yc(k, carry):
            b = zblock(k)
            ag_desc(u, buf, rows, b, ypeer, agy_s.at[u, b]).wait_send()
            ag_desc(u, buf, rows, b, cpeer, agc_s.at[u, b]).wait_send()
            b = yblock(k)
            ag_desc(u, buf, rows, b, cpeer, agc_s.at[u, b]).wait_send()
            return carry

        lax.fori_loop(0, planes, yc, 0)

    def a2a_desc(owner, to):
        return remote(
            hid_t.at[pl.ds(pl.multiple_of(to * part, part), part)],
            feats.at[:, pl.ds(pl.multiple_of(owner * tok, tok), tok)],
            a2a_s.at[to], a2a_r.at[owner], to,
        )

    barrier = pltpu.get_barrier_semaphore()
    peers(lambda p: pl.semaphore_signal(barrier, inc=1, device_id={"dp": p}, device_id_type=MESH))

    span = PER * tok

    def group_q(g):
        return qs[g * span:(g + 1) * span]

    for g in range(GROUPS):
        q = group_q(g)
        gram[g * HD:(g + 1) * HD] = mm(q, q, ((0,), (0,)))

    pl.semaphore_wait(barrier, n - 1)
    phase1_start(0, gram)

    def turn(k, carry):
        at = pl.multiple_of(k * HD, HD)
        hid_t[pl.ds(at, HD)] = hid[:, pl.ds(at, HD)].T
        return carry

    lax.fori_loop(0, feat // HD, turn, 0)
    peers(lambda p: a2a_desc(me, p).start())
    feats[:, pl.ds(pl.multiple_of(me * tok, tok), tok)] = hid_t[
        pl.ds(pl.multiple_of(me * part, part), part)
    ]

    row = lax.rem(lax.broadcasted_iota(jnp.int32, (span, tok), 0), tok)
    causal = row >= lax.broadcasted_iota(jnp.int32, (span, tok), 1)

    def forward(down, ups):
        step = min(1024, feat)

        def one(k, acc):
            at = pl.multiple_of(k * step, step)
            return acc + mm(hid[:, pl.ds(at, step)], down[pl.ds(at, step)])

        acc = lax.fori_loop(0, feat // step, one, jnp.zeros((tok, WIDTH), F32))
        latent_b[...] = acc.astype(BF16)
        errs = []
        for g in range(GROUPS):
            cols = slice(g * HD, (g + 1) * HD)
            recon = mm(latent_b[:, cols], ups[g])
            errs.append((keys[:, cols].astype(F32) - recon).astype(BF16))
        return errs

    def local_scores(errs, g):
        s = mm(group_q(g), errs[g], ((1,), (1,)))
        return jnp.where(causal, s, 0.0)

    def errors_grad(g, errs, local):
        hi, lo = split(finals[0, g * HD:(g + 1) * HD])
        cross = mm(errs[g], hi) + mm(errs[g], lo)
        return (pair_scale * (local + cross)).astype(BF16)

    def gradients(errs, locals_, ups, gl, upl):
        for g in range(GROUPS):
            cols = slice(g * HD, (g + 1) * HD)
            ge = errors_grad(g, errs, locals_[g])
            lg = (-mm(ge, ups[g], ((1,), (1,)))).astype(BF16)
            gl[pl.ds(pl.multiple_of(me * tok, tok), tok), cols] = lg
            upl[cols] = -mm(latent_b[:, cols], ge, ((0,), (0,)))

    def new_rows(old, gl):
        step = 1024

        def one(k, acc):
            at = pl.multiple_of(k * step, step)
            return acc + mm(feats[:, pl.ds(at, step)], gl[pl.ds(at, step)])

        acc = lax.fori_loop(0, total // step, one, jnp.zeros((part, WIDTH), F32))
        return (old.astype(F32) - RATE_DOWN * root * acc).astype(BF16)

    def new_up(old, u, g):
        grad = finals[u, g * HD:(g + 1) * HD]
        return (old.astype(F32) - RATE_UP * root * grad).astype(BF16)

    mine = pl.ds(pl.multiple_of(me * part, part), part)

    ups = [up0[g] for g in range(GROUPS)]
    errs = forward(down0, ups)
    phase2_start(0, gram, "suffix")
    locals_ = []
    for g in range(GROUPS):
        s = local_scores(errs, g).astype(BF16)
        locals_.append(mm(s, group_q(g), ((0,), (0,))))
    phase2_wait(0)
    gradients(errs, locals_, ups, gl1, upl1)
    phase1_start(1, upl1)
    gather(0, gl1, tok)
    peers(lambda p: a2a_desc(p, p).wait_recv())
    phase2_start(1, upl1, "sum")
    down1[mine] = new_rows(down0[mine], gl1)
    gather(1, down1, part)
    phase2_wait(1)

    ups = [new_up(up0[g], 1, g) for g in range(GROUPS)]
    errs = forward(down1, ups)
    for g in range(GROUPS):
        kgram[g * HD:(g + 1) * HD] = mm(errs[g], errs[g], ((0,), (0,)))
    phase1_start(2, kgram)
    locals_ = []
    sums = jnp.zeros((tok, 1), F32)
    for g in range(GROUPS):
        s = local_scores(errs, g)
        own = jnp.sum(s * s, axis=1, keepdims=True)
        for h in range(PER):
            sums = sums + own[h * tok:(h + 1) * tok]
        locals_.append(mm(s.astype(BF16), group_q(g), ((0,), (0,))))
    gradients(errs, locals_, ups, gl2, upl2)
    phase1_start(3, upl2)
    phase2_start(2, kgram, "prefix")
    gather(2, gl2, tok)
    phase2_start(3, upl2, "sum")
    rows_out[...] = new_rows(down1[mine], gl2)
    phase2_wait(2)
    for g in range(GROUPS):
        q = group_q(g)
        hi, lo = split(finals[2, g * HD:(g + 1) * HD])
        moved = mm(q, hi) + mm(q, lo)
        far = jnp.sum(moved * q.astype(F32), axis=1, keepdims=True)
        for h in range(PER):
            sums = sums + far[h * tok:(h + 1) * tok]
    where = (me * tok + 1 + lax.broadcasted_iota(jnp.int32, (tok, 1), 0)).astype(F32)
    err_out[...] = sums / (where * HEADS)
    phase2_wait(3)
    for g in range(GROUPS):
        up_out[g] = new_up(ups[g], 3, g)

    peers(lambda p: a2a_desc(me, p).wait_send())
    exchange_sends_done(0, gram)
    exchange_sends_done(1, upl1)
    exchange_sends_done(2, kgram)
    exchange_sends_done(3, upl2)
    gather_sends_done(0, gl1, tok)
    gather_sends_done(1, down1, part)
    gather_sends_done(2, gl2, tok)


def shards(hidden_rows, queries, keys, down_basis, up_basis, head_group):
    tok, feat = hidden_rows.shape
    n = lax.axis_size("dp")
    part = feat // n
    piece = WIDTH // n
    heads = jnp.arange(HEADS, dtype=jnp.int32)
    same = head_group[:, None] == head_group[None, :]
    before = jnp.sum((same & (heads[None, :] < heads[:, None])).astype(jnp.int32), axis=1)
    place = head_group * PER + before
    order = jnp.sum(jnp.where(place[None, :] == heads[:, None], heads[None, :], 0), axis=1)
    vmem = pl.BlockSpec(memory_space=pltpu.VMEM)
    dma = pltpu.SemaphoreType.DMA
    qs = pl.pallas_call(
        sort_heads,
        out_shape=jax.ShapeDtypeStruct((HEADS * tok, HD), BF16),
        in_specs=[pl.BlockSpec(memory_space=pltpu.SMEM), vmem],
        out_specs=vmem,
    )(order, queries)
    rows, up, err = pl.pallas_call(
        functools.partial(kernel, n, tok, feat),
        out_shape=(
            jax.ShapeDtypeStruct((part, WIDTH), BF16),
            jax.ShapeDtypeStruct((GROUPS, HD, HD), BF16),
            jax.ShapeDtypeStruct((tok, 1), F32),
        ),
        in_specs=[vmem] * 5,
        out_specs=(vmem, vmem, vmem),
        scratch_shapes=[
            pltpu.VMEM((feat, tok), BF16),
            pltpu.VMEM((part, n * tok), BF16),
            pltpu.VMEM((tok, WIDTH), BF16),
            pltpu.VMEM((n * tok, WIDTH), BF16),
            pltpu.VMEM((n * tok, WIDTH), BF16),
            pltpu.VMEM((feat, WIDTH), BF16),
            pltpu.VMEM((WIDTH, HD), F32),
            pltpu.VMEM((WIDTH, HD), F32),
            pltpu.VMEM((WIDTH, HD), F32),
            pltpu.VMEM((WIDTH, HD), F32),
            pltpu.VMEM((4, n, piece, HD), F32),
            pltpu.VMEM((4, n, piece, HD), F32),
            pltpu.VMEM((4, WIDTH, HD), F32),
            dma((n,)), dma((n,)),
            dma((4, n)), dma((4, n)), dma((4, n)), dma((4, n)),
            dma((3, n // 4)), dma((3, n)), dma((3, n)), dma((3, n)),
        ],
        compiler_params=pltpu.CompilerParams(
            collective_id=0, has_side_effects=True, vmem_limit_bytes=48 * 1024 * 1024
        ),
    )(hidden_rows, qs, keys, down_basis, up_basis)
    return rows, up, err.reshape(tok)


def solution(mesh):
    return jax.shard_map(
        shards,
        mesh=mesh,
        in_specs=(
            P(("parts", "dp"), None),
            P(("parts", "dp"), None),
            P(("parts", "dp"), None),
            P("parts", None),
            P("parts", None, None),
            P(),
        ),
        out_specs=(P(("parts", "dp"), None), P("parts", None, None), P(("parts", "dp"))),
        check_vma=False,
    )
```

time: 600 us -> 180 us (0.30)
  waiting for transfers between devices: 488 us -> 0 us
  Pallas kernels: 0 us -> 171 us
  matrix products: 60 us -> 0 us
  other arithmetic: 21.9 us -> 2.83 us
  between operations: 14.4 us -> 0.64 us
  local copies, waits for them, and re-layouts: 13.2 us -> 5.61 us
    reduce_scatter x2 -> x0, waiting for transfers between devices: 177 us -> none  [update(): lax.psum_scatter(full_term, 'dp', scatter_dimension=0, tiled=True)]
    psum x2 -> x0, waiting for transfers between devices: 172 us -> none  [update(): up_grad = lax.psum(up_local, 'dp')]
    pallas_call x0 -> x2, Pallas kernels: none -> 171 us  [the longest x1 168 us: shards(): pl.pallas_call(functools.partial(kernel, n, tok, feat), out_shape=(jax.Sh...]
    all_gather x3 -> x0, waiting for transfers between devices: 139 us -> none  [the longest x1 54.8 us: shards(): down_one = lax.all_gather(rows_one, 'dp', axis=0, tiled=True)]
    dot_general x28 -> x0, matrix products: 60 us -> none  [the longest x4 18.4 us: one_block(): jnp.einsum('ihd,jhd->hij', q_heads, e_heads, preferred_element_type=jnp.f...]
    add x27 -> x1, other arithmetic: 15.2 us -> 0.66 us  [shards(): place = head_group * PER + before]
  transfers between devices with their start and end apart: 7 -> 0, of which waited for: 7 -> 0; matrix products, arithmetic and copies ran while one was open for 9% -> 0% of each run, Pallas kernels for 0% -> 0%
where the time goes in v1:
time: 180 us
  Pallas kernels  171 us (95%)
  local copies, waits for them, and re-layouts  5.61 us (3%)
  other arithmetic  2.83 us (2%)
    pallas_call x1, Pallas kernels, shards(): pl.pallas_call(functools.partial(kernel, n, tok, feat), out_shape=(jax.Sh...  168 us
    unnamed x10, local copies, waits for them, and re-layouts  5.61 us

profile of v1, /device:TPU:0, one launch (start us, length us, event | category | flops | bytes accessed | tf_op | source)
XLA Modules:
  0.0 180.0 jit_solution(15155643122136159739)
XLA Ops:
  0.6 0.9 convert_reduce_fusion
  1.5 0.7 multiply_add_fusion
  2.2 0.6 select_reduce_fusion.order
  2.8 2.5 %shard_map.85.qs = bf16[4096,128]{1,0:T(8,128)(2,1)} custom-call(s32[32]{0:T(128)} %select_reduce_fusion.order, bf16[128,4096]{1,0:T(8,128)(2,1)} %queries.1), custom_call_target="tpu_custom_call" | custom-call | tf_op jit(solution)/shard_map/pallas_call | solution.py:347
  5.3 0.0 copy-start
  5.3 1.2 copy-done
  6.6 0.0 copy-start.1
  6.6 1.2 copy-done.1
  7.8 0.0 copy-start.2
  7.8 0.9 copy-done.2
  8.7 0.0 copy-start.3
  8.7 0.9 copy-done.3
  9.6 168.4 %shard_map.86 = (bf16[256,512]{1,0:T(8,128)(2,1)S(1)}, bf16[4,128,128]{2,1,0:T(8,128)(2,1)S(1)}, f32[128,1]{1,0:T(8,128)S(1)}) custom-call(bf16[128,4096]{1,0:T(8,128)(2,1)S(1)} %copy-done.1, bf16[4096,128]{1,0:T(8,128)(2,1)S(1)} %copy-done, bf16[128,512]{1,0:T(8,128)(2,1)S(1)} %copy-done.2, bf16[4096,512]{1,0:T(8,128)(2,1)} %down0.1, ...), custom_call_target="tpu_custom_call" | custom-call | tf_op jit(solution)/shard_map/pallas_call | solution.py:353
  178.0 0.6 reduce
  178.6 0.7 copy.11
  179.3 0.7 copy.12
Async XLA Ops:
  5.3 1.2 copy-start
  6.6 1.2 copy-start.1
  7.8 0.9 copy-start.2
  8.7 0.9 copy-start.3

commit v2 on v1

v2 whole, which is shorter than its diff:
```python
import functools
import math

import jax
import jax.numpy as jnp
from jax import lax
from jax.experimental import pallas as pl
from jax.experimental.pallas import tpu as pltpu
from jax.sharding import PartitionSpec as P

HEADS = 32
GROUPS = 4
HD = 128
PER = HEADS // GROUPS
WIDTH = GROUPS * HD
CHUNK = 64
RATE_DOWN = 1.0
RATE_UP = 8.0
F32 = jnp.float32
BF16 = jnp.bfloat16
MESH = pl.DeviceIdType.MESH


def mm(a, b, dims=((1,), (0,))):
    return lax.dot_general(a, b, (dims, ((), ())), preferred_element_type=F32)


def sort_heads(order, queries, qs):
    tok = queries.shape[0]
    for s in range(HEADS):
        col = pl.multiple_of(order[s] * HD, HD)
        qs[s * tok:(s + 1) * tok] = queries[:, pl.ds(col, HD)]


def kernel(
    n, tok, feat,
    hid, qs, keys, down0, up0,
    rows_out, up_out, err_out,
    hid_t, feats, latent_b, gl1, gl2, down1, gram, kgram, upl1, upl2,
    stages, results, finals,
    a2a_s, a2a_r, p1_s, p1_r, p2_s, p2_r, agz_s, agy_s, agc_s, agc_r, ag_r,
):
    me = lax.axis_index("dp")
    planes = n // 4
    zi, yi, ci = me // 4, lax.rem(me // 2, 2), lax.rem(me, 2)
    ypeer = zi * 4 + (1 - yi) * 2 + ci
    cpeer = zi * 4 + yi * 2 + (1 - ci)
    part = feat // n
    owners = min(n, WIDTH // 16)
    piece = WIDTH // owners
    total = n * tok
    pair_scale = 2.0 / (total * total * HEADS)
    root = math.sqrt(total)

    def remote(src, dst, s, r, to):
        return pltpu.make_async_remote_copy(
            src_ref=src, dst_ref=dst, send_sem=s, recv_sem=r,
            device_id={"dp": to}, device_id_type=MESH,
        )

    def many(ref, sem):
        return remote(ref, ref, sem, sem, cpeer)

    def peers(body):
        def one(k, carry):
            body(lax.rem(me + k, n))
            return carry

        lax.fori_loop(1, n, one, 0)

    def owning(p, body):
        if owners == n:
            body()
        else:
            pl.when(p < owners)(body)

    def phase1_desc(u, src, owner, to):
        return remote(
            src.at[pl.ds(pl.multiple_of(to * piece, piece), piece)],
            stages.at[u, owner], p1_s.at[u], p1_r.at[u], to,
        )

    def phase1_start(u, src):
        peers(lambda p: owning(p, lambda: phase1_desc(u, src, me, p).start()))

        def keep():
            stages[u, me] = src[pl.ds(pl.multiple_of(me * piece, piece), piece)]

        owning(me, keep)

    def phase2_desc(u, owner, to):
        return remote(
            results.at[u, to],
            finals.at[u, pl.ds(pl.multiple_of(owner * piece, piece), piece)],
            p2_s.at[u], p2_r.at[u], to,
        )

    def phase2_start(u, src, mode):
        def own():
            many(stages.at[u, pl.ds(0, n - 1)], p1_r.at[u]).wait_recv()
            zero = jnp.zeros((piece, HD), F32)
            if mode == "sum":
                tot = lax.fori_loop(0, n, lambda k, a: a + stages[u, k].astype(F32), zero)

                def put(k, carry):
                    results[u, k] = tot.astype(BF16)
                    return carry

                lax.fori_loop(0, n, put, 0)
            else:
                def scan(k, a):
                    at = n - 1 - k if mode == "suffix" else k
                    results[u, at] = a.astype(BF16)
                    return a + stages[u, at].astype(F32)

                lax.fori_loop(0, n, scan, zero)
            peers(lambda p: phase2_desc(u, me, p).start())
            finals[u, pl.ds(pl.multiple_of(me * piece, piece), piece)] = results[u, me]

        owning(me, own)

    def by_owners(ref, sem, act):
        def of(count):
            return lambda: act(many(ref.at[pl.ds(0, count * piece)], sem))

        if owners == n:
            of(n - 1)()
        else:
            pl.when(me < owners)(of(owners - 1))
            pl.when(me >= owners)(of(owners))

    def phase2_wait(u):
        by_owners(finals.at[u], p2_r.at[u], lambda c: c.wait_recv())

    def exchange_sends_done(u, src):
        by_owners(src, p1_s.at[u], lambda c: c.wait_send())
        owning(me, lambda: many(results.at[u, pl.ds(0, n - 1)], p2_s.at[u]).wait_send())

    def chunk_desc(u, buf, b, j, per, send, recv, to):
        ref = buf.at[pl.ds(pl.multiple_of((b * per + j) * CHUNK, CHUNK), CHUNK)]
        return remote(ref, ref, send, recv, to)

    def loop(lo, hi, body):
        def one(k, carry):
            body(k)
            return carry

        lax.fori_loop(lo, hi, one, 0)

    def gather(u, buf, rows):
        per = rows // CHUNK

        def got(z, y, j):
            sem = ag_r.at[u, (z * 2 + y) * per + j]
            b = z * 4 + y * 2 + ci
            chunk_desc(u, buf, b, j, per, agy_s.at[u], sem, ypeer).wait_recv()

        def go(send, z, y, j, to):
            sem = ag_r.at[u, (z * 2 + y) * per + j]
            chunk_desc(u, buf, z * 4 + y * 2 + ci, j, per, send, sem, to).start()

        def to_core(z, y, j):
            b = z * 4 + y * 2 + ci
            chunk_desc(u, buf, b, j, per, agc_s.at[u], agc_r.at[u], cpeer).start()

        def up(z, j):
            pl.when(zi < planes - 1)(lambda: go(agz_s.at[u, z * per + j], z, yi, j, me + 4))

        def down(z, j):
            at = (planes + z) * per + j
            pl.when(zi > 0)(lambda: go(agz_s.at[u, at], z, yi, j, me - 4))

        def across(z, j):
            go(agy_s.at[u], z, yi, j, ypeer)
            to_core(z, yi, j)

        def own(j):
            up(zi, j)
            down(zi, j)
            across(zi, j)

        loop(0, per, own)

        def from_y(z, j):
            got(z, 1 - yi, j)
            to_core(z, 1 - yi, j)

        def away(d):
            def one(j):
                @pl.when(zi - d >= 0)
                def _():
                    got(zi - d, yi, j)
                    up(zi - d, j)
                    across(zi - d, j)

                @pl.when(zi + d < planes)
                def _():
                    got(zi + d, yi, j)
                    down(zi + d, j)
                    across(zi + d, j)

            loop(0, per, one)

        def far_y(d):
            def one(j):
                pl.when(zi - d >= 0)(lambda: from_y(zi - d, j))
                pl.when(zi + d < planes)(lambda: from_y(zi + d, j))

            loop(0, per, one)

        def each(d):
            away(d)
            pl.when(d == 1)(lambda: loop(0, per, lambda j: from_y(zi, j)))
            pl.when(d > 1)(lambda: far_y(d - 1))

        loop(1, planes, each)
        far_y(planes - 1)
        many(buf.at[pl.ds(0, n // 2 * rows)], agc_r.at[u]).wait_recv()

    def gather_sends_done(u, buf, rows):
        per = rows // CHUNK

        def z_done(at):
            chunk_desc(u, buf, 0, 0, per, agz_s.at[u, at], agc_r.at[u], ypeer).wait_send()

        def one(k):
            z = k // per
            pl.when((zi < planes - 1) & (z <= zi))(lambda: z_done(k))
            pl.when((zi > 0) & (z >= zi))(lambda: z_done(planes * per + k))

        loop(0, planes * per, one)
        many(buf.at[pl.ds(0, n // 4 * rows)], agy_s.at[u]).wait_send()
        many(buf.at[pl.ds(0, n // 2 * rows)], agc_s.at[u]).wait_send()

    def a2a_desc(owner, to):
        return remote(
            hid_t.at[pl.ds(pl.multiple_of(to * part, part), part)],
            feats.at[:, pl.ds(pl.multiple_of(owner * tok, tok), tok)],
            a2a_s, a2a_r, to,
        )

    barrier = pltpu.get_barrier_semaphore()
    peers(lambda p: pl.semaphore_signal(barrier, inc=1, device_id={"dp": p}, device_id_type=MESH))

    span = PER * tok

    def group_q(g):
        return qs[g * span:(g + 1) * span]

    for g in range(GROUPS):
        q = group_q(g)
        gram[g * HD:(g + 1) * HD] = mm(q, q, ((0,), (0,))).astype(BF16)

    pl.semaphore_wait(barrier, n - 1)
    phase1_start(0, gram)

    def turn(k, carry):
        at = pl.multiple_of(k * HD, HD)
        hid_t[pl.ds(at, HD)] = hid[:, pl.ds(at, HD)].T
        return carry

    lax.fori_loop(0, feat // HD, turn, 0)
    peers(lambda p: a2a_desc(me, p).start())
    feats[:, pl.ds(pl.multiple_of(me * tok, tok), tok)] = hid_t[
        pl.ds(pl.multiple_of(me * part, part), part)
    ]

    row = lax.rem(lax.broadcasted_iota(jnp.int32, (span, tok), 0), tok)
    causal = row >= lax.broadcasted_iota(jnp.int32, (span, tok), 1)

    def forward(down, ups):
        step = min(1024, feat)

        def one(k, acc):
            at = pl.multiple_of(k * step, step)
            return acc + mm(hid[:, pl.ds(at, step)], down[pl.ds(at, step)])

        acc = lax.fori_loop(0, feat // step, one, jnp.zeros((tok, WIDTH), F32))
        latent_b[...] = acc.astype(BF16)
        errs = []
        for g in range(GROUPS):
            cols = slice(g * HD, (g + 1) * HD)
            recon = mm(latent_b[:, cols], ups[g])
            errs.append((keys[:, cols].astype(F32) - recon).astype(BF16))
        return errs

    def local_scores(errs, g):
        s = mm(group_q(g), errs[g], ((1,), (1,)))
        return jnp.where(causal, s, 0.0)

    def errors_grad(g, errs, local):
        cross = mm(errs[g], finals[0, g * HD:(g + 1) * HD])
        return (pair_scale * (local + cross)).astype(BF16)

    def gradients(errs, locals_, ups, gl, upl):
        for g in range(GROUPS):
            cols = slice(g * HD, (g + 1) * HD)
            ge = errors_grad(g, errs, locals_[g])
            lg = (-mm(ge, ups[g], ((1,), (1,)))).astype(BF16)
            gl[pl.ds(pl.multiple_of(me * tok, tok), tok), cols] = lg
            upl[cols] = (-mm(latent_b[:, cols], ge, ((0,), (0,)))).astype(BF16)

    def new_rows(old, gl):
        step = 1024

        def one(k, acc):
            at = pl.multiple_of(k * step, step)
            return acc + mm(feats[:, pl.ds(at, step)], gl[pl.ds(at, step)])

        acc = lax.fori_loop(0, total // step, one, jnp.zeros((part, WIDTH), F32))
        return (old.astype(F32) - RATE_DOWN * root * acc).astype(BF16)

    def new_up(old, u, g):
        grad = finals[u, g * HD:(g + 1) * HD].astype(F32)
        return (old.astype(F32) - RATE_UP * root * grad).astype(BF16)

    mine = pl.ds(pl.multiple_of(me * part, part), part)

    ups = [up0[g] for g in range(GROUPS)]
    errs = forward(down0, ups)
    phase2_start(0, gram, "suffix")
    locals_ = []
    for g in range(GROUPS):
        s = local_scores(errs, g).astype(BF16)
        locals_.append(mm(s, group_q(g), ((0,), (0,))))
    phase2_wait(0)
    gradients(errs, locals_, ups, gl1, upl1)
    phase1_start(1, upl1)
    gather(0, gl1, tok)
    many(feats.at[:, pl.ds(0, total - tok)], a2a_r).wait_recv()
    phase2_start(1, upl1, "sum")
    down1[mine] = new_rows(down0[mine], gl1)
    gather(1, down1, part)
    phase2_wait(1)

    ups = [new_up(up0[g], 1, g) for g in range(GROUPS)]
    errs = forward(down1, ups)
    for g in range(GROUPS):
        kgram[g * HD:(g + 1) * HD] = mm(errs[g], errs[g], ((0,), (0,))).astype(BF16)
    phase1_start(2, kgram)
    locals_ = []
    sums = jnp.zeros((tok, 1), F32)
    for g in range(GROUPS):
        s = local_scores(errs, g)
        own = jnp.sum(s * s, axis=1, keepdims=True)
        for h in range(PER):
            sums = sums + own[h * tok:(h + 1) * tok]
        locals_.append(mm(s.astype(BF16), group_q(g), ((0,), (0,))))
    gradients(errs, locals_, ups, gl2, upl2)
    phase1_start(3, upl2)
    phase2_start(2, kgram, "prefix")
    gather(2, gl2, tok)
    phase2_start(3, upl2, "sum")
    rows_out[...] = new_rows(down1[mine], gl2)
    phase2_wait(2)
    for g in range(GROUPS):
        q = group_q(g)
        moved = mm(q, finals[2, g * HD:(g + 1) * HD])
        far = jnp.sum(moved * q.astype(F32), axis=1, keepdims=True)
        for h in range(PER):
            sums = sums + far[h * tok:(h + 1) * tok]
    where = (me * tok + 1 + lax.broadcasted_iota(jnp.int32, (tok, 1), 0)).astype(F32)
    err_out[...] = sums / (where * HEADS)
    phase2_wait(3)
    for g in range(GROUPS):
        up_out[g] = new_up(ups[g], 3, g)

    many(hid_t.at[pl.ds(0, feat - part)], a2a_s).wait_send()
    exchange_sends_done(0, gram)
    exchange_sends_done(1, upl1)
    exchange_sends_done(2, kgram)
    exchange_sends_done(3, upl2)
    gather_sends_done(0, gl1, tok)
    gather_sends_done(1, down1, part)
    gather_sends_done(2, gl2, tok)


def shards(hidden_rows, queries, keys, down_basis, up_basis, head_group):
    tok, feat = hidden_rows.shape
    n = lax.axis_size("dp")
    part = feat // n
    piece = WIDTH // min(n, WIDTH // 16)
    chunks = max(feat, n * tok) // CHUNK
    heads = jnp.arange(HEADS, dtype=jnp.int32)
    same = head_group[:, None] == head_group[None, :]
    before = jnp.sum((same & (heads[None, :] < heads[:, None])).astype(jnp.int32), axis=1)
    place = head_group * PER + before
    order = jnp.sum(jnp.where(place[None, :] == heads[:, None], heads[None, :], 0), axis=1)
    vmem = pl.BlockSpec(memory_space=pltpu.VMEM)
    dma = pltpu.SemaphoreType.DMA
    qs = pl.pallas_call(
        sort_heads,
        out_shape=jax.ShapeDtypeStruct((HEADS * tok, HD), BF16),
        in_specs=[pl.BlockSpec(memory_space=pltpu.SMEM), vmem],
        out_specs=vmem,
    )(order, queries)
    rows, up, err = pl.pallas_call(
        functools.partial(kernel, n, tok, feat),
        out_shape=(
            jax.ShapeDtypeStruct((part, WIDTH), BF16),
            jax.ShapeDtypeStruct((GROUPS, HD, HD), BF16),
            jax.ShapeDtypeStruct((tok, 1), F32),
        ),
        in_specs=[vmem] * 5,
        out_specs=(vmem, vmem, vmem),
        scratch_shapes=[
            pltpu.VMEM((feat, tok), BF16),
            pltpu.VMEM((part, n * tok), BF16),
            pltpu.VMEM((tok, WIDTH), BF16),
            pltpu.VMEM((n * tok, WIDTH), BF16),
            pltpu.VMEM((n * tok, WIDTH), BF16),
            pltpu.VMEM((feat, WIDTH), BF16),
            pltpu.VMEM((WIDTH, HD), BF16),
            pltpu.VMEM((WIDTH, HD), BF16),
            pltpu.VMEM((WIDTH, HD), BF16),
            pltpu.VMEM((WIDTH, HD), BF16),
            pltpu.VMEM((4, n, piece, HD), BF16),
            pltpu.VMEM((4, n, piece, HD), BF16),
            pltpu.VMEM((4, WIDTH, HD), BF16),
            dma, dma,
            dma((4,)), dma((4,)), dma((4,)), dma((4,)),
            dma((3, chunks // 2)), dma((3,)), dma((3,)), dma((3,)), dma((3, chunks // 2)),
        ],
        compiler_params=pltpu.CompilerParams(
            collective_id=0, has_side_effects=True, vmem_limit_bytes=48 * 1024 * 1024
        ),
    )(hidden_rows, qs, keys, down_basis, up_basis)
    return rows, up, err.reshape(tok)


def solution(mesh):
    return jax.shard_map(
        shards,
        mesh=mesh,
        in_specs=(
            P(("parts", "dp"), None),
            P(("parts", "dp"), None),
            P(("parts", "dp"), None),
            P("parts", None),
            P("parts", None, None),
            P(),
        ),
        out_specs=(P(("parts", "dp"), None), P("parts", None, None), P(("parts", "dp"))),
        check_vma=False,
    )
```

time: 180 us -> 127 us (0.71)
  Pallas kernels: 171 us -> 118 us
    pallas_call x1, Pallas kernels: 168 us -> 115 us  [shards(): pl.pallas_call(functools.partial(kernel, n, tok, feat), out_shape=(jax.Sh...]
where the time goes in v2:
time: 127 us
  Pallas kernels  118 us (93%)
  local copies, waits for them, and re-layouts  5.61 us (4%)
  other arithmetic  2.83 us (2%)
    pallas_call x1, Pallas kernels, shards(): pl.pallas_call(functools.partial(kernel, n, tok, feat), out_shape=(jax.Sh...  115 us
    unnamed x10, local copies, waits for them, and re-layouts  5.61 us

profile of v2, /device:TPU:0, one launch (start us, length us, event | category | flops | bytes accessed | tf_op | source)
XLA Modules:
  0.0 126.9 jit_solution(13855942044007110761)
XLA Ops:
  0.6 0.9 convert_reduce_fusion
  1.5 0.7 multiply_add_fusion
  2.2 0.6 select_reduce_fusion.order
  2.8 2.5 %shard_map.85.qs = bf16[4096,128]{1,0:T(8,128)(2,1)} custom-call(s32[32]{0:T(128)} %select_reduce_fusion.order, bf16[128,4096]{1,0:T(8,128)(2,1)} %queries.1), custom_call_target="tpu_custom_call" | custom-call | tf_op jit(solution)/shard_map/pallas_call | solution.py:391
  5.3 0.0 copy-start
  5.3 1.2 copy-done
  6.6 0.0 copy-start.1
  6.6 1.2 copy-done.1
  7.8 0.0 copy-start.2
  7.8 0.9 copy-done.2
  8.7 0.0 copy-start.3
  8.7 0.9 copy-done.3
  9.6 115.3 %shard_map.86 = (bf16[256,512]{1,0:T(8,128)(2,1)S(1)}, bf16[4,128,128]{2,1,0:T(8,128)(2,1)S(1)}, f32[128,1]{1,0:T(8,128)S(1)}) custom-call(bf16[128,4096]{1,0:T(8,128)(2,1)S(1)} %copy-done.1, bf16[4096,128]{1,0:T(8,128)(2,1)S(1)} %copy-done, bf16[128,512]{1,0:T(8,128)(2,1)S(1)} %copy-done.2, bf16[4096,512]{1,0:T(8,128)(2,1)} %down0.1, ...), custom_call_target="tpu_custom_call" | custom-call | tf_op jit(solution)/shard_map/pallas_call | solution.py:397
  124.9 0.6 reduce
  125.5 0.7 copy.11
  126.2 0.7 copy.12
Async XLA Ops:
  5.3 1.2 copy-start
  6.6 1.2 copy-start.1
  7.8 0.9 copy-start.2
  8.7 0.9 copy-start.3

commit v3 on v2

--- a/solution.py
+++ b/solution.py
@@ -37,7 +37,7 @@
     hid, qs, keys, down0, up0,
     rows_out, up_out, err_out,
     hid_t, feats, latent_b, gl1, gl2, down1, gram, kgram, upl1, upl2,
-    stages, results, finals,
+    stages_gram, stages_up, results, finals,
     a2a_s, a2a_r, p1_s, p1_r, p2_s, p2_r, agz_s, agy_s, agc_s, agc_r, ag_r,
 ):
     me = lax.axis_index("dp")
@@ -74,17 +74,20 @@
         else:
             pl.when(p < owners)(body)
 
+    def stage(u):
+        return (stages_up if u % 2 else stages_gram).at[u // 2]
+
     def phase1_desc(u, src, owner, to):
         return remote(
             src.at[pl.ds(pl.multiple_of(to * piece, piece), piece)],
-            stages.at[u, owner], p1_s.at[u], p1_r.at[u], to,
+            stage(u).at[owner], p1_s.at[u], p1_r.at[u], to,
         )
 
     def phase1_start(u, src):
         peers(lambda p: owning(p, lambda: phase1_desc(u, src, me, p).start()))
 
         def keep():
-            stages[u, me] = src[pl.ds(pl.multiple_of(me * piece, piece), piece)]
+            stage(u)[me] = src[pl.ds(pl.multiple_of(me * piece, piece), piece)]
 
         owning(me, keep)
 
@@ -97,13 +100,16 @@
 
     def phase2_start(u, src, mode):
         def own():
-            many(stages.at[u, pl.ds(0, n - 1)], p1_r.at[u]).wait_recv()
+            many(stage(u).at[pl.ds(0, n - 1)], p1_r.at[u]).wait_recv()
             zero = jnp.zeros((piece, HD), F32)
-            if mode == "sum":
-                tot = lax.fori_loop(0, n, lambda k, a: a + stages[u, k].astype(F32), zero)
+            if u % 2:
+                tot = lax.fori_loop(0, n, lambda k, a: a + stage(u)[k].astype(F32), zero)
+
+                old = mode[pl.ds(pl.multiple_of(me * piece, piece), piece)].astype(F32)
+                new = (old - RATE_UP * root * tot).astype(BF16)
 
                 def put(k, carry):
-                    results[u, k] = tot.astype(BF16)
+                    results[u, k] = new
                     return carry
 
                 lax.fori_loop(0, n, put, 0)
@@ -111,7 +117,7 @@
                 def scan(k, a):
                     at = n - 1 - k if mode == "suffix" else k
                     results[u, at] = a.astype(BF16)
-                    return a + stages[u, at].astype(F32)
+                    return a + stage(u)[at].astype(F32)
 
                 lax.fori_loop(0, n, scan, zero)
             peers(lambda p: phase2_desc(u, me, p).start())
@@ -260,7 +266,6 @@
         return carry
 
     lax.fori_loop(0, feat // HD, turn, 0)
-    peers(lambda p: a2a_desc(me, p).start())
     feats[:, pl.ds(pl.multiple_of(me * tok, tok), tok)] = hid_t[
         pl.ds(pl.multiple_of(me * part, part), part)
     ]
@@ -310,15 +315,12 @@
         acc = lax.fori_loop(0, total // step, one, jnp.zeros((part, WIDTH), F32))
         return (old.astype(F32) - RATE_DOWN * root * acc).astype(BF16)
 
-    def new_up(old, u, g):
-        grad = finals[u, g * HD:(g + 1) * HD].astype(F32)
-        return (old.astype(F32) - RATE_UP * root * grad).astype(BF16)
-
     mine = pl.ds(pl.multiple_of(me * part, part), part)
 
-    ups = [up0[g] for g in range(GROUPS)]
+    ups = [up0[g * HD:(g + 1) * HD] for g in range(GROUPS)]
     errs = forward(down0, ups)
     phase2_start(0, gram, "suffix")
+    peers(lambda p: a2a_desc(me, p).start())
     locals_ = []
     for g in range(GROUPS):
         s = local_scores(errs, g).astype(BF16)
@@ -328,12 +330,12 @@
     phase1_start(1, upl1)
     gather(0, gl1, tok)
     many(feats.at[:, pl.ds(0, total - tok)], a2a_r).wait_recv()
-    phase2_start(1, upl1, "sum")
+    phase2_start(1, upl1, up0)
     down1[mine] = new_rows(down0[mine], gl1)
     gather(1, down1, part)
     phase2_wait(1)
 
-    ups = [new_up(up0[g], 1, g) for g in range(GROUPS)]
+    ups = [finals[1, g * HD:(g + 1) * HD] for g in range(GROUPS)]
     errs = forward(down1, ups)
     for g in range(GROUPS):
         kgram[g * HD:(g + 1) * HD] = mm(errs[g], errs[g], ((0,), (0,))).astype(BF16)
@@ -350,7 +352,7 @@
     phase1_start(3, upl2)
     phase2_start(2, kgram, "prefix")
     gather(2, gl2, tok)
-    phase2_start(3, upl2, "sum")
+    phase2_start(3, upl2, finals.at[1])
     rows_out[...] = new_rows(down1[mine], gl2)
     phase2_wait(2)
     for g in range(GROUPS):
@@ -362,8 +364,7 @@
     where = (me * tok + 1 + lax.broadcasted_iota(jnp.int32, (tok, 1), 0)).astype(F32)
     err_out[...] = sums / (where * HEADS)
     phase2_wait(3)
-    for g in range(GROUPS):
-        up_out[g] = new_up(ups[g], 3, g)
+    up_out[...] = finals[3]
 
     many(hid_t.at[pl.ds(0, feat - part)], a2a_s).wait_send()
     exchange_sends_done(0, gram)
@@ -398,7 +399,7 @@
         functools.partial(kernel, n, tok, feat),
         out_shape=(
             jax.ShapeDtypeStruct((part, WIDTH), BF16),
-            jax.ShapeDtypeStruct((GROUPS, HD, HD), BF16),
+            jax.ShapeDtypeStruct((WIDTH, HD), BF16),
             jax.ShapeDtypeStruct((tok, 1), F32),
         ),
         in_specs=[vmem] * 5,
@@ -414,7 +415,8 @@
             pltpu.VMEM((WIDTH, HD), BF16),
             pltpu.VMEM((WIDTH, HD), BF16),
             pltpu.VMEM((WIDTH, HD), BF16),
-            pltpu.VMEM((4, n, piece, HD), BF16),
+            pltpu.VMEM((2, n, piece, HD), BF16),
+            pltpu.VMEM((2, n, piece, HD), BF16),
             pltpu.VMEM((4, n, piece, HD), BF16),
             pltpu.VMEM((4, WIDTH, HD), BF16),
             dma, dma,
@@ -424,8 +426,8 @@
         compiler_params=pltpu.CompilerParams(
             collective_id=0, has_side_effects=True, vmem_limit_bytes=48 * 1024 * 1024
         ),
-    )(hidden_rows, qs, keys, down_basis, up_basis)
-    return rows, up, err.reshape(tok)
+    )(hidden_rows, qs, keys, down_basis, up_basis.reshape(WIDTH, HD))
+    return rows, up.reshape(GROUPS, HD, HD), err.reshape(tok)
 
 
 def solution(mesh):

time: 127 us -> 126 us (level)
    pallas_call x1, Pallas kernels: 115 us -> 114 us  [shards(): pl.pallas_call(functools.partial(kernel, n, tok, feat), out_shape=(jax.Sh...]
where the time goes in v3:
time: 126 us
  Pallas kernels  117 us (93%)
  local copies, waits for them, and re-layouts  5.61 us (4%)
  other arithmetic  2.83 us (2%)
    pallas_call x1, Pallas kernels, shards(): pl.pallas_call(functools.partial(kernel, n, tok, feat), out_shape=(jax.Sh...  114 us
    unnamed x10, local copies, waits for them, and re-layouts  5.61 us

profile of v3, /device:TPU:0, one launch (start us, length us, event | category | flops | bytes accessed | tf_op | source)
XLA Modules:
  0.0 125.6 jit_solution(2343586493852315589)
XLA Ops:
  0.6 0.9 convert_reduce_fusion
  1.5 0.7 multiply_add_fusion
  2.2 0.6 select_reduce_fusion.order
  2.8 2.5 %shard_map.85.qs = bf16[4096,128]{1,0:T(8,128)(2,1)} custom-call(s32[32]{0:T(128)} %select_reduce_fusion.order, bf16[128,4096]{1,0:T(8,128)(2,1)} %queries.1), custom_call_target="tpu_custom_call" | custom-call | tf_op jit(solution)/shard_map/pallas_call | solution.py:392
  5.3 0.0 copy-start
  5.3 1.2 copy-done
  6.6 0.0 copy-start.1
  6.6 1.2 copy-done.1
  7.8 0.0 copy-start.2
  7.8 0.9 copy-done.2
  8.7 0.0 copy-start.3
  8.7 0.9 copy-done.3
  9.6 114.0 %shard_map.86 = (bf16[256,512]{1,0:T(8,128)(2,1)S(1)}, bf16[512,128]{1,0:T(8,128)(2,1)S(1)}, f32[128,1]{1,0:T(8,128)S(1)}) custom-call(bf16[128,4096]{1,0:T(8,128)(2,1)S(1)} %copy-done.1, bf16[4096,128]{1,0:T(8,128)(2,1)S(1)} %copy-done, bf16[128,512]{1,0:T(8,128)(2,1)S(1)} %copy-done.2, bf16[4096,512]{1,0:T(8,128)(2,1)} %down0.1, bf16[512,128]{1,0:T(8,128)(2,1)S(1)} %bitcast.2), custom_call_target="tpu_custom_call" | custom-call | tf_op jit(solution)/shard_map/pallas_call | solution.py:398
  123.6 0.6 reduce
  124.2 0.7 copy.11
  124.9 0.7 copy.12
Async XLA Ops:
  5.3 1.2 copy-start
  6.6 1.2 copy-start.1
  7.8 0.9 copy-start.2
  8.7 0.9 copy-start.3

commit v4 on v3

--- a/solution.py
+++ b/solution.py
@@ -348,9 +348,9 @@
         for h in range(PER):
             sums = sums + own[h * tok:(h + 1) * tok]
         locals_.append(mm(s.astype(BF16), group_q(g), ((0,), (0,))))
+    phase2_start(2, kgram, "prefix")
     gradients(errs, locals_, ups, gl2, upl2)
     phase1_start(3, upl2)
-    phase2_start(2, kgram, "prefix")
     gather(2, gl2, tok)
     phase2_start(3, upl2, finals.at[1])
     rows_out[...] = new_rows(down1[mine], gl2)

time: 126 us -> 128 us (1.016)
  Pallas kernels: 117 us -> 119 us
    pallas_call x1, Pallas kernels: 114 us -> 116 us  [shards(): pl.pallas_call(functools.partial(kernel, n, tok, feat), out_shape=(jax.Sh...]
where the time goes in v4:
time: 128 us
  Pallas kernels  119 us (93%)
  local copies, waits for them, and re-layouts  5.61 us (4%)
  other arithmetic  2.83 us (2%)
    pallas_call x1, Pallas kernels, shards(): pl.pallas_call(functools.partial(kernel, n, tok, feat), out_shape=(jax.Sh...  116 us
    unnamed x10, local copies, waits for them, and re-layouts  5.61 us

profile of v4, /device:TPU:0, one launch (start us, length us, event | category | flops | bytes accessed | tf_op | source)
XLA Modules:
  0.0 127.8 jit_solution(13644548330484081122)
XLA Ops:
  0.6 0.9 convert_reduce_fusion
  1.5 0.7 multiply_add_fusion
  2.2 0.6 select_reduce_fusion.order
  2.8 2.5 %shard_map.85.qs = bf16[4096,128]{1,0:T(8,128)(2,1)} custom-call(s32[32]{0:T(128)} %select_reduce_fusion.order, bf16[128,4096]{1,0:T(8,128)(2,1)} %queries.1), custom_call_target="tpu_custom_call" | custom-call | tf_op jit(solution)/shard_map/pallas_call | solution.py:392
  5.3 0.0 copy-start
  5.3 1.2 copy-done
  6.6 0.0 copy-start.1
  6.6 1.2 copy-done.1
  7.8 0.0 copy-start.2
  7.8 0.9 copy-done.2
  8.7 0.0 copy-start.3
  8.7 0.9 copy-done.3
  9.6 116.2 %shard_map.86 = (bf16[256,512]{1,0:T(8,128)(2,1)S(1)}, bf16[512,128]{1,0:T(8,128)(2,1)S(1)}, f32[128,1]{1,0:T(8,128)S(1)}) custom-call(bf16[128,4096]{1,0:T(8,128)(2,1)S(1)} %copy-done.1, bf16[4096,128]{1,0:T(8,128)(2,1)S(1)} %copy-done, bf16[128,512]{1,0:T(8,128)(2,1)S(1)} %copy-done.2, bf16[4096,512]{1,0:T(8,128)(2,1)} %down0.1, bf16[512,128]{1,0:T(8,128)(2,1)S(1)} %bitcast.2), custom_call_target="tpu_custom_call" | custom-call | tf_op jit(solution)/shard_map/pallas_call | solution.py:398
  125.8 0.6 reduce
  126.4 0.7 copy.11
  127.1 0.7 copy.12
Async XLA Ops:
  5.3 1.2 copy-start
  6.6 1.2 copy-start.1
  7.8 0.9 copy-start.2
  8.7 0.9 copy-start.3
